TPU v7x, 512 devices: a whole 4x4x16 slice. The times are simulated.
512 devices in a mesh: dp: 128 (over y, z, core), helper: 4 (over x).
Axes of the slice: x: 4, y: 4, z: 16, core: 2. Of those that a mesh axis runs over, the one named last changes fastest.
Arguments:
- embeddings: bfloat16 [131072, 768], P(('dp', 'helper')), may hold values from -70 to 70
- cluster: int32 [131072], P(('dp', 'helper')), may hold values from 0 to 127, as said below
- order_rank: int32 [131072], P(('dp', 'helper')), may hold values from 0 to 1023
Outputs:
- nearest_earlier: float32 [131072], P(('dp', 'helper'))
Inputs may be any that keep to these rules, and one draw needn't show every extreme that they name: Among the rows of one device at most 4 name the same cluster; in every draw one cluster is named by exactly 4 rows of every device.
All inputs are finite; a program needn't handle non-finite values.
Results may differ from a plain program's by a relative error of at most 0.00053.
Values may be sent and summed in bfloat16 or wider, within the bound.
A program may use at most 64 MiB of HBM per device.

v0:
```python
from functools import reduce

import jax
import jax.numpy as jnp
from jax import lax
from jax.sharding import PartitionSpec as P

sentinel = 2147483647
block_rows = 512


def unit_rows(raw_rows):
    values = raw_rows.astype(jnp.float32)
    return (values * lax.rsqrt(jnp.sum(values * values, axis=-1, keepdims=True) + 1e-06)).astype(
        jnp.bfloat16
    )


def masked_best(query_units, query_keys, other_units, other_keys):
    results = []
    for first_row in range(0, other_units.shape[0], block_rows):
        last_row = min(first_row + block_rows, other_units.shape[0])
        score_values = jnp.einsum(
            "qd,kd->qk",
            query_units,
            other_units[first_row:last_row],
            preferred_element_type=jnp.float32,
        )
        earlier = other_keys[None, first_row:last_row] < query_keys[:, None]
        results.append(jnp.max(jnp.where(earlier, score_values, jnp.float32(-1.0)), axis=1))
    return reduce(jnp.maximum, results)


def body(embeddings, cluster, order_rank):
    rows_dev = embeddings.shape[0]
    feature_count = embeddings.shape[1]
    owners = lax.axis_size("dp")
    helpers = lax.axis_size("helper")
    total_rows = rows_dev * owners * helpers
    slot_count = 2 * rows_dev // owners
    device_at = lax.axis_index("dp") * helpers + lax.axis_index("helper")
    row_ids = device_at * rows_dev + jnp.arange(rows_dev, dtype=jnp.int32)
    order_key = order_rank * total_rows + row_ids
    onehot = (cluster[:, None] == jnp.arange(owners, dtype=jnp.int32)[None, :]).astype(jnp.int32)
    before = jnp.cumsum(onehot, axis=0) - onehot
    position = jnp.sum(before * onehot, axis=1)
    target = cluster * slot_count + position
    send_rows = (
        jnp.zeros((owners * slot_count, feature_count), jnp.bfloat16).at[target].set(embeddings)
    )
    send_keys = jnp.full((owners * slot_count,), sentinel, jnp.int32).at[target].set(order_key)
    panel_rows, panel_keys = (
        lax.all_to_all(send_rows, "dp", split_axis=0, concat_axis=0, tiled=True),
        lax.all_to_all(send_keys, "dp", split_axis=0, concat_axis=0, tiled=True),
    )
    panel_units = unit_rows(panel_rows)
    panel_count = panel_keys.shape[0]
    nearest = jnp.maximum(
        jnp.full((panel_count,), -1.0, jnp.float32),
        masked_best(
            panel_units,
            panel_keys,
            lax.all_gather(panel_units, "helper", axis=0, tiled=True),
            lax.all_gather(panel_keys, "helper", axis=0, tiled=True),
        ),
    )
    returned = lax.all_to_all(nearest, "dp", split_axis=0, concat_axis=0, tiled=True)
    return returned[target]


def solution(mesh):
    return jax.shard_map(
        body,
        mesh=mesh,
        in_specs=(P(("dp", "helper"), None), P(("dp", "helper")), P(("dp", "helper"))),
        out_specs=P(("dp", "helper")),
        check_vma=False,
    )
```

profile of v0, /device:TPU:1, one launch (start us, length us, event | category | flops | bytes accessed | tf_op | source)
XLA Modules:
  0.0 165.1 jit_solution(18248901659385886942)
XLA Ops:
  6.5 0.8 copy.6
  7.3 0.2 fusion.10
  7.6 0.9 fusion.12
  8.5 0.7 compare_select_fusion
  9.2 2.3 %scatter_custom_fusion.1 = bf16[512,768]{1,0:T(8,128)(2,1)S(1)} fusion(s32[256]{0:T(256)S(1)} %get-tuple-element.9, bf16[256,768]{1,0:T(8,128)(2,1)} %param.3, bf16[]{:T(256)} %constant.11.clone.1), kind=kCustom, calls=%fused_computation.17 | custom fusion | bytes 786944 | tf_op jit(solution)/shard_map/scatter | solution.py:49
  11.5 0.2 all_to_all.23
  11.7 63.9 %all_to_all.30 = bf16[128,4,768]{2,1,0:T(4,128)(2,1)S(1)} all-to-all(bf16[128,4,768]{2,1,0:T(4,128)(2,1)S(1)} %all_to_all.23), channel_id=1, replica_groups=mesh['dp'=128,'helper'=4] {'dp'}, dimensions={0} | all-to-all | bytes 1572864 | tf_op jit(solution)/shard_map/all_to_all | solution.py:53
  75.6 0.5 multiply_reduce_fusion
  76.1 0.1 rsqrt.12
  76.2 0.1 reshape.89
  76.3 1.0 multiply_convert_fusion
  77.4 1.4 scatter_custom_fusion
  78.8 0.1 all_to_all.20
  78.9 22.9 %all_to_all.31 = s32[128,4,1]{1,2,0:T(1,128)S(1)} all-to-all(s32[128,4,1]{1,2,0:T(1,128)S(1)} %bitcast.32), channel_id=1, replica_groups=mesh['dp'=128,'helper'=4] {'dp'}, dimensions={0} | all-to-all | bytes 4096 | tf_op jit(solution)/shard_map/all_to_all | solution.py:54
  101.8 0.1 all_to_all.22
  101.9 0.5 broadcast.61
  102.4 0.8 reduce.9
  103.2 0.1 reshape.117
  103.4 9.5 %all-gather = s32[4,1,512]{2,1,0:T(1,128)S(1)} all-gather(s32[1,1,512]{2,1,0:T(1,128)S(1)} %reshape.117), channel_id=1, replica_groups=mesh['dp'=128,'helper'=4] {'helper'}, dimensions={0}, use_global_device_ids=true | all-gather | bytes 10240 | tf_op jit(solution)/shard_map/all_gather | solution.py:64
  112.8 4.8 %all-gather.3.cloned.1.call-done = bf16[2048,768]{1,0:T(8,128)(2,1)} async-done(((bf16[512,768]{1,0:T(8,128)(2,1)}), bf16[2048,768]{1,0:T(8,128)(2,1)}) %all-gather.3.cloned.1.call-update) | async-done | bytes 3145744 | tf_op jit(solution)/shard_map/all_gather | solution.py:63
  117.7 2.1 %fusion.3 = f32[512]{0:T(512)S(1)} fusion(bf16[512,768]{1,0:T(8,128)(2,1)} %multiply_convert_fusion, bf16[2048,768]{1,0:T(8,128)(2,1)} %all-gather.3.cloned.1.call-done, s32[512]{0:T(512)S(1)} %all_to_all.22, s32[512]{0:T(512)S(1)} %bitcast.38), kind=kOutput, calls=%fused_computation.12 | convolution fusion | flops 403439104 | bytes 1579008 | tf_op jit(solution)/shard_map/qd,kd->qk/dot_general | solution.py:23
  119.8 0.2 copy-done.1
  120.0 0.6 fusion.2
  120.7 0.6 fusion.1
  121.3 0.6 fusion
  121.9 0.7 max_broadcast_in_dim.14
  122.6 16.6 %all-to-all-start.2 = ((f32[128,4,1]{1,2,0:T(1,128)}), f32[128,4,1]{1,2,0:T(1,128)S(1)}, u32[]{:S(2)}, u32[]{:S(2)}) async-start(f32[128,4,1]{1,2,0:T(1,128)} %bitcast.9), calls=%async_computation.2 | async-start | bytes 131072 | tf_op jit(solution)/shard_map/all_to_all | solution.py:67
  139.3 15.0 %all-to-all-done.2 = f32[128,4,1]{1,2,0:T(1,128)S(1)} async-done(((f32[128,4,1]{1,2,0:T(1,128)}), f32[128,4,1]{1,2,0:T(1,128)S(1)}, u32[]{:S(2)}, u32[]{:S(2)}) %all-to-all-start.2) | async-done | bytes 2080 | tf_op jit(solution)/shard_map/all_to_all | solution.py:67
  154.3 0.5 broadcast.62
  154.8 0.8 reduce.10
  155.6 0.1 all_to_all.26
  155.7 2.5 %gather_fusion = f32[256]{0:T(256)} fusion(f32[512]{0:T(512)S(1)} %all_to_all.26, s32[1024]{0:T(1024)S(1)} %pad_clamp_fusion), kind=kCustom, calls=%fused_computation | custom fusion | bytes 3072 | tf_op jit(solution)/shard_map/gather | solution.py:68
  (15 shorter events, 0.1 us)
Async XLA Ops:
  6.5 111.1 %all-gather.3.cloned.1.call-start = ((), (), s32[]{:S(2)}) async-start(), calls=%async_computation.3 | async-start | bytes 3932160 | tf_op jit(solution)/shard_map/all_gather | solution.py:63
  77.3 42.5 %copy-start = (bf16[512,768]{1,0:T(8,128)(2,1)S(1)}, bf16[512,768]{1,0:T(8,128)(2,1)}, u32[]{:S(2)}) copy-start(bf16[512,768]{1,0:T(8,128)(2,1)} %multiply_convert_fusion) | copy-start | bytes 2359300
  117.7 2.4 %copy-start.1 = (bf16[2048,768]{1,0:T(8,128)(2,1)S(1)}, bf16[2048,768]{1,0:T(8,128)(2,1)}, u32[]{:S(2)}) copy-start(bf16[2048,768]{1,0:T(8,128)(2,1)} %all-gather.3.cloned.1.call-done) | copy-start | bytes 9437188
  122.6 31.6 %all-to-all-start.2 = ((f32[128,4,1]{1,2,0:T(1,128)}), f32[128,4,1]{1,2,0:T(1,128)S(1)}, u32[]{:S(2)}, u32[]{:S(2)}) async-start(f32[128,4,1]{1,2,0:T(1,128)} %bitcast.9), calls=%async_computation.2 | async-start | bytes 131072 | tf_op jit(solution)/shard_map/all_to_all | solution.py:67
Sparse Core Ops, SparseCore 0:
  77.5 40.1 all-gather.2
where the time goes:
time: 165 us
  blocking collectives  96.3 us (58%)
  waiting for transfers between devices  19.8 us (12%)
  starting transfers between devices  16.6 us (10%)
  between operations  13.5 us (8%)
  local copies, waits for them, and re-layouts  9.83 us (6%)
  other arithmetic  4.97 us (3%)
  matrix products  3.99 us (2%)
    all_to_all x1, blocking collectives, body(): lax.all_to_all(send_rows, 'dp', split_axis=0, concat_axis=0, tiled=True)  63.9 us
    all_to_all x1, blocking collectives, body(): lax.all_to_all(send_keys, 'dp', split_axis=0, concat_axis=0, tiled=True)  22.9 us
    all_to_all x1, starting transfers between devices, body(): lax.all_to_all(nearest, 'dp', split_axis=0, concat_axis=0, tiled=True)  16.6 us
    all_to_all x1, waiting for transfers between devices, body(): lax.all_to_all(nearest, 'dp', split_axis=0, concat_axis=0, tiled=True)  15 us
    all_gather x1, blocking collectives, body(): lax.all_gather(panel_keys, 'helper', axis=0, tiled=True)  9.48 us
    all_gather x1, waiting for transfers between devices, body(): lax.all_gather(panel_units, 'helper', axis=0, tiled=True)  4.84 us
    dot_general x4, matrix products, masked_best(): jnp.einsum('qd,kd->qk', query_units, other_units[first_row:last_row], pre...  3.99 us
  transfers between devices with their start and end apart: 2, of which 2 were waited for; matrix products, arithmetic and copies ran while one was open for 2% of the time, Pallas kernels for 0%

commit v1 on v0

v1 whole, which is shorter than its diff:
```python
import functools

import jax
import jax.numpy as jnp
from jax import lax
from jax.experimental import pallas as pl
from jax.experimental.pallas import tpu as pltpu
from jax.sharding import PartitionSpec as P

MESH = pl.DeviceIdType.MESH
Y, Z, CORES, X = 4, 16, 2, 4
SLOTS = 4
BLOCK = CORES * SLOTS
ROWS_Z = Y * BLOCK
PANEL = Z * ROWS_Z
GROUP = 2
GROUPS = Z // GROUP
EMPTY = 8388608.0


def z_offset(index):
    return (index + 1) // 2 if index % 2 else -(index // 2)


def wait_bytes(ref, sem):
    pltpu.make_async_copy(ref, ref, sem).wait()


def iota(shape, dim):
    return lax.broadcasted_iota(jnp.int32, shape, dim)


def dot_t(lhs, rhs):
    return lax.dot_general(lhs, rhs, (((1,), (1,)), ((), ())), preferred_element_type=jnp.float32)


def kernel(
    emb_ref,
    cluster_ref,
    rank_ref,
    out_ref,
    units,
    meta,
    send_z,
    from_z,
    panels,
    key_send,
    key_z,
    key_y,
    key_x,
    key_cols,
    result,
    ret_z,
    ret_y,
    core_send,
    core_recv,
    z_send,
    z_recv,
    y_send,
    y_recv,
    x_send,
    x1_recv,
    x2_recv,
    x3_recv,
    key_send_sem,
    key_recv_sem,
    ret_send_sem,
    ret_recv_sem,
):
    dp, hx = lax.axis_index("dp"), lax.axis_index("helper")
    core, chip = dp % CORES, dp // CORES
    y, z = chip // Z, chip % Z

    def at(dy=0, dz=0, dx=0, dcore=0):
        chip_to = ((y + dy + Y) % Y) * Z + (z + dz + Z) % Z
        return (chip_to * CORES + (core + dcore) % CORES, (hx + dx + X) % X)

    def remote(src, dst, send_sem, recv_sem, to):
        pltpu.make_async_remote_copy(
            src_ref=src,
            dst_ref=dst,
            send_sem=send_sem,
            recv_sem=recv_sem,
            device_id=to,
            device_id_type=MESH,
        ).start()

    barrier = pltpu.get_barrier_semaphore()
    peers = [at(dz=z_offset(a)) for a in range(Z - 1, 0, -1)]
    peers += [at(dy=d) for d in range(1, Y)] + [at(dy=d, dcore=1) for d in range(Y)]
    peers += [at(dx=d) for d in range(1, X)]
    for peer in peers:
        pl.semaphore_signal(barrier, inc=1, device_id=peer, device_id_type=MESH)

    rows = emb_ref.shape[0]
    values = emb_ref[...].astype(jnp.float32)
    scale = lax.rsqrt(jnp.sum(values * values, axis=-1, keepdims=True) + 1e-06)
    units[core] = (values * scale).astype(jnp.bfloat16)

    cluster = cluster_ref[...].reshape(1, rows)
    rank = rank_ref[...].reshape(1, rows)
    across = jnp.broadcast_to(cluster, (rows, rows))
    down = jnp.transpose(across)
    same_before = (down == across) & (iota((rows, rows), 0) < iota((rows, rows), 1))
    slot = jnp.sum(same_before.astype(jnp.float32), axis=0, keepdims=True).astype(jnp.int32)
    owner_chip = cluster // CORES
    dy = (owner_chip // Z - y + Y) % Y
    dz = (owner_chip % Z - z + Z) % Z
    a_of = jnp.where(dz == 0, 0, jnp.where(dz <= Z // 2, 2 * dz - 1, 2 * (Z - dz)))
    target = a_of * ROWS_Z + dy * BLOCK + core * SLOTS + slot
    owner_core = cluster % CORES
    key = rank * (Z * Y * CORES * X * SLOTS) + (dp * X + hx) * SLOTS + slot + 1
    meta[core, 0:1, :] = (target + owner_core * PANEL).astype(jnp.float32)
    meta[core, 1:2, :] = (key // 16384).astype(jnp.float32)
    meta[core, 2:3, :] = (key // 128 % 128).astype(jnp.float32)
    meta[core, 3:4, :] = (key % 128).astype(jnp.float32)
    meta[core, 4:8, :] = jnp.zeros((4, rows), jnp.float32)

    pl.semaphore_wait(barrier, len(peers))
    remote(units.at[core], units.at[core], core_send.at[0], core_recv.at[0], at(dcore=1))
    remote(meta.at[core], meta.at[core], core_send.at[1], core_recv.at[1], at(dcore=1))
    wait_bytes(meta.at[0], core_recv.at[1])
    wait_bytes(units.at[0], core_recv.at[0])

    targets = [meta[c, 0:1, :].astype(jnp.int32) - core * PANEL for c in range(CORES)]
    chunk = 4 * ROWS_Z
    for first in range(Z - 4, -1, -4):
        picked = jnp.zeros((chunk, units.shape[2]), jnp.float32)
        for c in range(CORES):
            pick = (iota((chunk, rows), 0) + first * ROWS_Z == targets[c]).astype(jnp.float32)
            picked += jnp.dot(
                pick.astype(jnp.bfloat16), units[c], preferred_element_type=jnp.float32
            )
        picked = picked.astype(jnp.bfloat16).reshape(4, Y, BLOCK, units.shape[2])
        for i in range(3, -1, -1):
            a = first + i
            if a == 0:
                from_z[0] = picked[0]
            else:
                send_z[a] = picked[i]
                remote(
                    send_z.at[a],
                    from_z.at[a],
                    z_send,
                    z_recv.at[a // GROUP],
                    at(dz=z_offset(a)),
                )

    keys = jnp.zeros((Z, 128), jnp.float32)
    lane = iota((128, rows), 0)
    for c in range(CORES):
        here = (targets[c] >= 0) & (targets[c] < PANEL)
        row_a = jnp.where(here, targets[c] // ROWS_Z, -1)
        pick = (iota((Z, rows), 0) == row_a).astype(jnp.float32).astype(jnp.bfloat16)
        part = jnp.where(
            lane < ROWS_Z,
            meta[c, 1:2, :],
            jnp.where(lane < 2 * ROWS_Z, meta[c, 2:3, :], meta[c, 3:4, :]),
        )
        part = jnp.where(
            (lane % ROWS_Z == targets[c] % ROWS_Z) & (lane < 3 * ROWS_Z), part, 0.0
        )
        keys += dot_t(pick, part.astype(jnp.bfloat16))
    key_send[...] = keys.reshape(Z, 1, 128)
    key_z[0] = keys[0:1]
    for a in range(Z - 1, 0, -1):
        remote(
            key_send.at[a],
            key_z.at[a],
            key_send_sem.at[0],
            key_recv_sem.at[0],
            at(dz=z_offset(a)),
        )
    wait_bytes(key_z.at[pl.ds(1, Z - 1)], key_recv_sem.at[0])
    for d in range(1, Y):
        remote(key_z, key_y.at[d], key_send_sem.at[1], key_recv_sem.at[1], at(dy=d))
    key_y[0] = key_z[...]
    wait_bytes(key_y.at[pl.ds(1, Y - 1)], key_recv_sem.at[1])
    lane = iota((Z, 128), 1)
    merged = jnp.zeros((Z, 128), jnp.float32)
    for d in range(Y):
        merged += jnp.where(lane % ROWS_Z // BLOCK == d, key_y[d].reshape(Z, 128), 0.0)
    merged = (
        merged * 16384.0
        + pltpu.roll(merged, 128 - ROWS_Z, 1) * 128.0
        + pltpu.roll(merged, 128 - 2 * ROWS_Z, 1)
    )
    key_x[0] = jnp.where(merged == 0.0, EMPTY, merged)
    for place, dx in ((1, 1), (2, X - 1), (3, 2)):
        remote(
            key_x.at[0], key_x.at[place], key_send_sem.at[2], key_recv_sem.at[2], at(dx=dx)
        )

    def group(g):
        return pl.ds(g * GROUP, GROUP)

    def forward(g):
        wait_bytes(panels.at[1, group(g)], x1_recv.at[g])
        wait_bytes(panels.at[2, group(g)], x2_recv.at[g])
        held, dx = (1, 1) if g % 2 else (2, -1)
        remote(
            panels.at[held, group(g)], panels.at[3, group(g)], x_send, x3_recv.at[g], at(dx=dx)
        )

    for g in range(GROUPS - 1, -1, -1):
        low = max(g * GROUP, 1)
        wait_bytes(from_z.at[pl.ds(low, (g + 1) * GROUP - low)], z_recv.at[g])
        for d in range(1, Y):
            remote(
                from_z.at[group(g), d],
                panels.at[0, group(g), d],
                y_send,
                y_recv.at[g],
                at(dy=d),
            )
        pltpu.make_async_copy(
            from_z.at[group(g), 0], panels.at[0, group(g), 0], y_recv.at[g]
        ).start()
        wait_bytes(panels.at[0, group(g)], y_recv.at[g])
        remote(panels.at[0, group(g)], panels.at[1, group(g)], x_send, x1_recv.at[g], at(dx=1))
        remote(panels.at[0, group(g)], panels.at[2, group(g)], x_send, x2_recv.at[g], at(dx=-1))
        if g == GROUPS - 1:
            wait_bytes(key_x.at[pl.ds(1, X - 1)], key_recv_sem.at[2])
            shape = (Z, ROWS_Z, 128)
            for p in range(X):
                spread = jnp.broadcast_to(key_x[p].reshape(Z, 1, 128), shape)
                column = jnp.sum(
                    jnp.where(iota(shape, 2) == iota(shape, 1), spread, 0.0),
                    axis=2,
                    keepdims=True,
                )
                key_cols[p] = jnp.broadcast_to(column, shape).reshape(PANEL, 128)
        else:
            forward(g + 1)
    forward(0)
    for g in range(GROUPS - 1, -1, -1):
        wait_bytes(panels.at[3, group(g)], x3_recv.at[g])

    width = units.shape[2]
    own_keys = jnp.transpose(key_cols[0])[0:1, :]
    half = Z // 2

    def tile(step, best):
        p, h = step // 2, step % 2
        own = panels[0].reshape(PANEL, width)
        others = panels[p, pl.ds(h * half, half)].reshape(half * ROWS_Z, width)
        scores = dot_t(others, own)
        other_keys = key_cols[p, pl.ds(h * half * ROWS_Z, half * ROWS_Z), :][:, 0:1]
        scores = jnp.where(other_keys < own_keys, scores, -1.0)
        return jnp.maximum(best, jnp.max(scores, axis=0, keepdims=True))

    best = lax.fori_loop(0, 2 * X, tile, jnp.full((1, PANEL), -1.0, jnp.float32))

    for i in range(PANEL // 128):
        result[i] = best[:, i * 128 : (i + 1) * 128]
    for a in range(Z - 1, 0, -1):
        remote(
            result.at[a // 4],
            ret_z.at[a],
            ret_send_sem.at[0],
            ret_recv_sem.at[0],
            at(dz=-z_offset(a)),
        )
    ret_z[0] = result[0]
    wait_bytes(ret_z.at[pl.ds(1, Z - 1)], ret_recv_sem.at[0])
    for d in range(Y):
        for other in range(CORES):
            if d or other:
                remote(
                    ret_z,
                    ret_y.at[core * Y + d],
                    ret_send_sem.at[1],
                    ret_recv_sem.at[1],
                    at(dy=-d, dcore=other),
                )
    ret_y[core * Y] = ret_z[...]
    wait_bytes(ret_y.at[pl.ds(1, CORES * Y - 1)], ret_recv_sem.at[1])
    table = []
    for c in range(CORES):
        merged = jnp.zeros((Z, 128), jnp.float32)
        for d in range(Y):
            merged += jnp.where(lane % ROWS_Z // BLOCK == d, ret_y[c * Y + d].reshape(Z, 128), 0.0)
        table.append(merged)
    table = jnp.concatenate(table, axis=0)
    code = meta[core, 0:1, :].astype(jnp.int32)
    spot = code % PANEL
    chosen = (iota((128, rows), 0) == spot % 128).astype(jnp.float32)
    found = jnp.dot(
        table, chosen, precision=lax.Precision.HIGHEST, preferred_element_type=jnp.float32
    )
    wanted = code // PANEL * Z + spot // ROWS_Z
    found = jnp.where(iota((CORES * Z, rows), 0) == wanted, found, 0.0)
    out_ref[...] = jnp.sum(found, axis=0, keepdims=True)

    wait_bytes(units.at[0], core_send.at[0])
    wait_bytes(meta.at[0], core_send.at[1])
    wait_bytes(from_z.at[pl.ds(1, Z - 1)], z_send)
    wait_bytes(panels.at[0, pl.ds(0, Z * (Y - 1) // Y)], y_send)
    wait_bytes(panels.at[pl.ds(1, X - 1)], x_send)
    wait_bytes(key_z.at[pl.ds(1, Z - 1)], key_send_sem.at[0])
    wait_bytes(key_y.at[pl.ds(1, Y - 1)], key_send_sem.at[1])
    wait_bytes(key_x.at[pl.ds(1, X - 1)], key_send_sem.at[2])
    wait_bytes(ret_z.at[pl.ds(1, Z - 1)], ret_send_sem.at[0])
    wait_bytes(ret_y.at[pl.ds(1, CORES * Y - 1)], ret_send_sem.at[1])


def body(embeddings, cluster, order_rank):
    rows, width = embeddings.shape
    vmem = pl.BlockSpec(memory_space=pltpu.VMEM)
    dma = pltpu.SemaphoreType.DMA
    found = pl.pallas_call(
        kernel,
        out_shape=jax.ShapeDtypeStruct((1, rows), jnp.float32),
        in_specs=[vmem] * 3,
        out_specs=vmem,
        scratch_shapes=[
            pltpu.VMEM((CORES, rows, width), jnp.bfloat16),
            pltpu.VMEM((CORES, 8, rows), jnp.float32),
            pltpu.VMEM((Z, Y, BLOCK, width), jnp.bfloat16),
            pltpu.VMEM((Z, Y, BLOCK, width), jnp.bfloat16),
            pltpu.VMEM((X, Z, Y, BLOCK, width), jnp.bfloat16),
            pltpu.VMEM((Z, 1, 128), jnp.float32),
            pltpu.VMEM((Z, 1, 128), jnp.float32),
            pltpu.VMEM((Y, Z, 1, 128), jnp.float32),
            pltpu.VMEM((X, Z, 128), jnp.float32),
            pltpu.VMEM((X, PANEL, 128), jnp.float32),
            pltpu.VMEM((PANEL // 128, 1, 128), jnp.float32),
            pltpu.VMEM((Z, 1, 128), jnp.float32),
            pltpu.VMEM((CORES * Y, Z, 1, 128), jnp.float32),
            dma((2,)),
            dma((2,)),
            dma,
            dma((GROUPS,)),
            dma,
            dma((GROUPS,)),
            dma,
            dma((GROUPS,)),
            dma((GROUPS,)),
            dma((GROUPS,)),
            dma((3,)),
            dma((3,)),
            dma((2,)),
            dma((2,)),
        ],
        compiler_params=pltpu.CompilerParams(
            collective_id=0, has_side_effects=True, vmem_limit_bytes=48 * 1024 * 1024
        ),
    )(embeddings, cluster, order_rank)
    return found.reshape(rows)


def solution(mesh):
    return jax.shard_map(
        body,
        mesh=mesh,
        in_specs=(P(("dp", "helper"), None), P(("dp", "helper")), P(("dp", "helper"))),
        out_specs=P(("dp", "helper")),
        check_vma=False,
    )
```

time: 165 us -> 122 us (0.74)
  Pallas kernels: 0 us -> 119 us
  blocking collectives: 96.3 us -> 0 us
  waiting for transfers between devices: 19.8 us -> 0 us
  starting transfers between devices: 16.6 us -> 0 us
  between operations: 13.5 us -> 0.01 us
  local copies, waits for them, and re-layouts: 9.83 us -> 2.92 us
  other arithmetic: 4.97 us -> 0 us
  matrix products: 3.99 us -> 0 us
    pallas_call x0 -> x1, Pallas kernels: none -> 119 us  [body(): pl.pallas_call(kernel, out_shape=jax.ShapeDtypeStruct((1, rows), jnp.floa...]
    all_to_all x2 -> x0, blocking collectives: 86.8 us -> none  [the longest x1 63.9 us: body(): lax.all_to_all(send_rows, 'dp', split_axis=0, concat_axis=0, tiled=True)]
    all_to_all x1 -> x0, starting transfers between devices: 16.6 us -> none  [body(): lax.all_to_all(nearest, 'dp', split_axis=0, concat_axis=0, tiled=True)]
    all_to_all x1 -> x0, waiting for transfers between devices: 15 us -> none  [body(): lax.all_to_all(nearest, 'dp', split_axis=0, concat_axis=0, tiled=True)]
    all_gather x1 -> x0, blocking collectives: 9.48 us -> none  [body(): lax.all_gather(panel_keys, 'helper', axis=0, tiled=True)]
    all_gather x1 -> x0, waiting for transfers between devices: 4.84 us -> none  [body(): lax.all_gather(panel_units, 'helper', axis=0, tiled=True)]
    dot_general x4 -> x0, matrix products: 3.99 us -> none  [masked_best(): jnp.einsum('qd,kd->qk', query_units, other_units[first_row:last_row], pre...]
    scatter x2 -> x0, local copies, waits for them, and re-layouts: 3.74 us -> none  [the longest x1 2.34 us: body(): jnp.zeros((owners * slot_count, feature_count), jnp.bfloat16).at[target]]
  transfers between devices with their start and end apart: 2 -> 0, of which waited for: 2 -> 0; matrix products, arithmetic and copies ran while one was open for 2% -> 0% of each run, Pallas kernels for 0% -> 0%
where the time goes in v1:
time: 122 us
  Pallas kernels  119 us (98%)
  local copies, waits for them, and re-layouts  2.92 us (2%)
    pallas_call x1, Pallas kernels, body(): pl.pallas_call(kernel, out_shape=jax.ShapeDtypeStruct((1, rows), jnp.floa...  119 us
    unnamed x7, local copies, waits for them, and re-layouts  2.92 us

profile of v1, /device:TPU:1, one launch (start us, length us, event | category | flops | bytes accessed | tf_op | source)
XLA Modules:
  0.0 122.0 jit_solution(17961491681675123907)
XLA Ops:
  0.0 0.0 copy-start
  0.0 1.0 copy-done
  1.0 0.0 copy-start.1
  1.0 0.7 copy-done.1
  1.7 0.0 copy-start.2
  1.7 0.7 copy-done.2
  2.4 119.1 %shard_map.37 = f32[1,256]{1,0:T(1,128)S(1)} custom-call(bf16[256,768]{1,0:T(8,128)(2,1)S(1)} %copy-done, s32[256]{0:T(256)S(1)} %copy-done.1, s32[256]{0:T(256)S(1)} %copy-done.2), custom_call_target="tpu_custom_call" | custom-call | tf_op jit(solution)/shard_map/pallas_call | solution.py:311
  121.4 0.6 copy.5
Async XLA Ops:
  0.0 1.0 copy-start
  1.0 0.7 copy-start.1
  1.7 0.7 copy-start.2

commit v2 on v1

v2 whole, which is shorter than its diff:
```python
import functools

import jax
import jax.numpy as jnp
from jax import lax
from jax.experimental import pallas as pl
from jax.experimental.pallas import tpu as pltpu
from jax.sharding import PartitionSpec as P

MESH = pl.DeviceIdType.MESH
Y, Z, CORES, X = 4, 16, 2, 4
SLOTS = 4
BLOCK = CORES * SLOTS
ROWS_Z = Y * BLOCK
PANEL = Z * ROWS_Z
SPANS = tuple((low, low + 2) for low in range(0, Z, 2))
GROUPS = len(SPANS)
PACE = (-1,) * GROUPS
KEY_STEP = 2
LAG_X = 1
HELD = 3
EMPTY = 8388608.0


def z_offset(index):
    return (index + 1) // 2 if index % 2 else -(index // 2)


def wait_bytes(ref, sem):
    pltpu.make_async_copy(ref, ref, sem).wait()


def iota(shape, dim):
    return lax.broadcasted_iota(jnp.int32, shape, dim)


def dot_t(lhs, rhs):
    return lax.dot_general(lhs, rhs, (((1,), (1,)), ((), ())), preferred_element_type=jnp.float32)


def kernel(
    emb_hbm,
    cluster_hbm,
    rank_hbm,
    out_ref,
    emb_ref,
    cluster_ref,
    rank_ref,
    units,
    send_z,
    from_z,
    landed,
    panels,
    key_send,
    key_z,
    key_y,
    key_x,
    key_cols,
    result,
    ret_z,
    ret_y,
    z_send,
    z_recv,
    y_send,
    y_recv,
    x_send,
    x1_recv,
    x2_recv,
    key_send_sem,
    key_recv_sem,
    ret_send_sem,
    ret_recv_sem,
    load_sem,
    far_send,
    far_recv,
    far_sem,
):
    dp, hx = lax.axis_index("dp"), lax.axis_index("helper")
    core, chip = dp % CORES, dp // CORES
    y, z = chip // Z, chip % Z

    def at(dy=0, dz=0, dx=0, dcore=0):
        chip_to = ((y + dy + Y) % Y) * Z + (z + dz + Z) % Z
        return (chip_to * CORES + (core + dcore) % CORES, (hx + dx + X) % X)

    def remote(src, dst, send_sem, recv_sem, to):
        pltpu.make_async_remote_copy(
            src_ref=src,
            dst_ref=dst,
            send_sem=send_sem,
            recv_sem=recv_sem,
            device_id=to,
            device_id_type=MESH,
        ).start()

    loads = [
        pltpu.make_async_copy(src, dst, load_sem.at[i])
        for i, (src, dst) in enumerate(
            ((cluster_hbm, cluster_ref), (rank_hbm, rank_ref), (emb_hbm, emb_ref))
        )
    ]
    for load in loads:
        load.start()
    barrier = pltpu.get_barrier_semaphore()
    peers = [at(dz=z_offset(a)) for a in range(Z - 1, 0, -1)]
    peers += [at(dy=d) for d in range(1, Y)] + [at(dy=d, dcore=1) for d in range(Y)]
    peers += [at(dx=1), at(dx=-1)]
    for peer in peers:
        pl.semaphore_signal(barrier, inc=1, device_id=peer, device_id_type=MESH)

    rows, width = emb_ref.shape
    loads[0].wait()
    loads[1].wait()
    cluster = cluster_ref[...].reshape(1, rows)
    rank = rank_ref[...].reshape(1, rows)
    across = jnp.broadcast_to(cluster, (rows, rows))
    down = jnp.transpose(across)
    same_before = (down == across) & (iota((rows, rows), 0) < iota((rows, rows), 1))
    slot = jnp.sum(same_before.astype(jnp.float32), axis=0, keepdims=True).astype(jnp.int32)
    owner_core, owner_chip = cluster % CORES, cluster // CORES
    dy = (owner_chip // Z - y + Y) % Y
    dz = (owner_chip % Z - z + Z) % Z
    a_of = jnp.where(dz == 0, 0, jnp.where(dz <= Z // 2, 2 * dz - 1, 2 * (Z - dz)))
    place = (owner_core * Y + dy) * SLOTS + slot
    target = a_of * ROWS_Z + place

    loads[2].wait()
    values = emb_ref[...].astype(jnp.float32)
    scale = lax.rsqrt(jnp.sum(values * values, axis=-1, keepdims=True) + 1e-06)
    units[...] = (values * scale).astype(jnp.bfloat16)
    chunk = 4 * ROWS_Z
    for first in range(0, Z, 4):
        pick = (iota((chunk, rows), 0) + first * ROWS_Z == target).astype(jnp.float32)
        picked = jnp.dot(
            pick.astype(jnp.bfloat16), units[...], preferred_element_type=jnp.float32
        )
        picked = picked.astype(jnp.bfloat16).reshape(4, CORES, Y, SLOTS, width)
        for i in range(4):
            if first + i:
                send_z[first + i] = picked[i]
            else:
                from_z[0] = picked[0]

    def group_of(a):
        return next(g for g, (low, high) in enumerate(SPANS) if low <= a < high)

    def release(arrived):
        for g, (low, high) in enumerate(SPANS):
            if PACE[g] == arrived:
                for a in range(max(low, 1), high):
                    send_rows(a)

    def send_rows(a):
        remote(
            send_z.at[a], from_z.at[a], z_send, z_recv.at[group_of(a)], at(dz=z_offset(a))
        )

    key = rank * (Z * Y * CORES * X * SLOTS) + (dp * X + hx) * SLOTS + slot + 1
    parts = [key // 16384, key // 128 % 128, key % 128]
    lane = iota((128, rows), 0)
    spread = jnp.where(
        lane < ROWS_Z, parts[0], jnp.where(lane < 2 * ROWS_Z, parts[1], parts[2])
    )
    spread = jnp.where((lane % ROWS_Z == place) & (lane < 3 * ROWS_Z), spread, 0)
    pick = (iota((Z, rows), 0) == a_of).astype(jnp.float32).astype(jnp.bfloat16)
    keys = dot_t(pick, spread.astype(jnp.float32).astype(jnp.bfloat16))
    key_send[...] = keys.reshape(Z, 1, 128)
    key_z[0] = keys[0:1]
    pl.semaphore_wait(barrier, len(peers))
    for a in range(1, Z):
        remote(
            key_send.at[a],
            key_z.at[a],
            key_send_sem.at[0],
            key_recv_sem.at[0],
            at(dz=z_offset(a)),
        )
    release(-1)
    lane = iota((Z, 128), 1)

    def keys_to_y():
        wait_bytes(key_z.at[pl.ds(1, Z - 1)], key_recv_sem.at[0])
        for d in range(Y):
            for other in range(CORES):
                if d or other:
                    remote(
                        key_z,
                        key_y.at[core * Y + d],
                        key_send_sem.at[1],
                        key_recv_sem.at[1],
                        at(dy=d, dcore=other),
                    )
        key_y[core * Y] = key_z[...]

    def keys_to_x():
        wait_bytes(key_y.at[pl.ds(1, CORES * Y - 1)], key_recv_sem.at[1])
        merged = jnp.zeros((Z, 128), jnp.float32)
        for c in range(CORES):
            for d in range(Y):
                shift = (128 + SLOTS * (d + c) - Y * SLOTS * core) % 128
                moved = pltpu.roll(key_y[c * Y + d].reshape(Z, 128), shift, 1)
                merged += jnp.where(lane % ROWS_Z // SLOTS == CORES * d + c, moved, 0.0)
        merged = (
            merged * 16384.0
            + pltpu.roll(merged, 128 - ROWS_Z, 1) * 128.0
            + pltpu.roll(merged, 128 - 2 * ROWS_Z, 1)
        )
        key_x[0] = jnp.where(merged == 0.0, EMPTY, merged)
        for place, dx in ((1, 1), (2, -1)):
            remote(
                key_x.at[0], key_x.at[place], key_send_sem.at[2], key_recv_sem.at[2], at(dx=dx)
            )

    def group(g):
        return pl.ds(SPANS[g][0], SPANS[g][1] - SPANS[g][0])

    def to_y(g):
        low, high = SPANS[g]
        low = max(low, 1)
        wait_bytes(from_z.at[pl.ds(low, high - low)], z_recv.at[g])
        release(g)
        for d in range(Y):
            for other in range(CORES):
                src = from_z.at[group(g), (core + other) % CORES, d]
                dst = landed.at[group(g), d, core]
                if d or other:
                    remote(src, dst, y_send, y_recv.at[g], at(dy=d, dcore=other))
                else:
                    pltpu.make_async_copy(src, dst, y_recv.at[g]).start()

    def to_x(g):
        wait_bytes(landed.at[group(g)], y_recv.at[g])
        panels[0, group(g)] = landed[group(g)].reshape(-1, Y, BLOCK, width)
        remote(panels.at[0, group(g)], panels.at[1, group(g)], x_send, x1_recv.at[g], at(dx=1))
        remote(panels.at[0, group(g)], panels.at[2, group(g)], x_send, x2_recv.at[g], at(dx=-1))

    def key_columns():
        wait_bytes(key_x.at[pl.ds(1, HELD - 1)], key_recv_sem.at[2])
        shape = (Z, ROWS_Z, 128)
        for p in range(HELD):
            spread = jnp.broadcast_to(key_x[p].reshape(Z, 1, 128), shape)
            column = jnp.sum(
                jnp.where(iota(shape, 2) == iota(shape, 1), spread, 0.0),
                axis=2,
                keepdims=True,
            )
            key_cols[p] = jnp.broadcast_to(column, shape).reshape(PANEL, 128)

    key_steps = {KEY_STEP: keys_to_y, KEY_STEP + 1: keys_to_x, KEY_STEP + 2: key_columns}
    for step in range(GROUPS + LAG_X):
        if step < GROUPS:
            to_y(step)
        if step >= LAG_X:
            to_x(step - LAG_X)
        if step in key_steps:
            key_steps[step]()

    half = Z // 2

    def arrived(low, high):
        for g, (first, last) in enumerate(SPANS):
            if low <= first < high:
                wait_bytes(panels.at[1, group(g)], x1_recv.at[g])
                wait_bytes(panels.at[2, group(g)], x2_recv.at[g])

    def largest(query, best, tiles):
        query_keys = jnp.transpose(key_cols[query])[0:1, :]

        def tile(step, best):
            p, h = tiles(step)
            queries = panels[query].reshape(PANEL, width)
            others = panels[p, pl.ds(h * half, half)].reshape(half * ROWS_Z, width)
            scores = dot_t(others, queries)
            other_keys = key_cols[p, pl.ds(h * half * ROWS_Z, half * ROWS_Z), :][:, 0:1]
            scores = jnp.where(other_keys < query_keys, scores, -1.0)
            return jnp.maximum(best, jnp.max(scores, axis=0, keepdims=True))

        return lambda count: lax.fori_loop(0, count, tile, best)

    none = jnp.full((1, PANEL), -1.0, jnp.float32)
    best = largest(0, none, lambda step: (0, step))(2)
    arrived(0, half)
    best = largest(0, best, lambda step: (1 + step, 0))(2)
    arrived(half, Z)
    far = largest(1, none, lambda step: (2, step))(2)
    for i in range(PANEL // 128):
        far_send[i] = far[:, i * 128 : (i + 1) * 128]
    remote(far_send, far_recv, far_sem.at[0], far_sem.at[1], at(dx=-1))
    best = largest(0, best, lambda step: (1 + step, 1))(2)
    wait_bytes(far_recv, far_sem.at[1])

    for i in range(PANEL // 128):
        result[i] = jnp.maximum(best[:, i * 128 : (i + 1) * 128], far_recv[i])
    for a in range(Z - 1, 0, -1):
        remote(
            result.at[a // 4],
            ret_z.at[a],
            ret_send_sem.at[0],
            ret_recv_sem.at[0],
            at(dz=-z_offset(a)),
        )
    ret_z[0] = result[0]
    wait_bytes(ret_z.at[pl.ds(1, Z - 1)], ret_recv_sem.at[0])
    for d in range(Y):
        for other in range(CORES):
            if d or other:
                remote(
                    ret_z,
                    ret_y.at[core * Y + d],
                    ret_send_sem.at[1],
                    ret_recv_sem.at[1],
                    at(dy=-d, dcore=other),
                )
    ret_y[core * Y] = ret_z[...]
    wait_bytes(ret_y.at[pl.ds(1, CORES * Y - 1)], ret_recv_sem.at[1])
    table = []
    for c in range(CORES):
        merged = jnp.zeros((Z, 128), jnp.float32)
        for d in range(Y):
            merged += jnp.where(lane % ROWS_Z // BLOCK == d, ret_y[c * Y + d].reshape(Z, 128), 0.0)
        table.append(merged)
    table = jnp.concatenate(table, axis=0)
    spot = a_of * ROWS_Z + dy * BLOCK + core * SLOTS + slot
    chosen = (iota((128, rows), 0) == spot % 128).astype(jnp.float32)
    found = jnp.dot(
        table, chosen, precision=lax.Precision.HIGHEST, preferred_element_type=jnp.float32
    )
    wanted = owner_core * Z + a_of
    found = jnp.where(iota((CORES * Z, rows), 0) == wanted, found, 0.0)
    out_ref[...] = jnp.sum(found, axis=0, keepdims=True)

    wait_bytes(from_z.at[pl.ds(1, Z - 1)], z_send)
    wait_bytes(landed.at[pl.ds(0, Z - Z // (Y * CORES))], y_send)
    wait_bytes(panels.at[pl.ds(1, HELD - 1)], x_send)
    wait_bytes(far_send, far_sem.at[0])
    wait_bytes(key_z.at[pl.ds(1, Z - 1)], key_send_sem.at[0])
    wait_bytes(key_y.at[pl.ds(1, CORES * Y - 1)], key_send_sem.at[1])
    wait_bytes(key_x.at[pl.ds(1, HELD - 1)], key_send_sem.at[2])
    wait_bytes(ret_z.at[pl.ds(1, Z - 1)], ret_send_sem.at[0])
    wait_bytes(ret_y.at[pl.ds(1, CORES * Y - 1)], ret_send_sem.at[1])


def body(embeddings, cluster, order_rank):
    rows, width = embeddings.shape
    vmem = pl.BlockSpec(memory_space=pltpu.VMEM)
    dma = pltpu.SemaphoreType.DMA
    found = pl.pallas_call(
        kernel,
        out_shape=jax.ShapeDtypeStruct((1, rows), jnp.float32),
        in_specs=[pl.BlockSpec(memory_space=pl.ANY)] * 3,
        out_specs=vmem,
        scratch_shapes=[
            pltpu.VMEM((rows, width), jnp.bfloat16),
            pltpu.VMEM((rows,), jnp.int32),
            pltpu.VMEM((rows,), jnp.int32),
            pltpu.VMEM((rows, width), jnp.bfloat16),
            pltpu.VMEM((Z, CORES, Y, SLOTS, width), jnp.bfloat16),
            pltpu.VMEM((Z, CORES, Y, SLOTS, width), jnp.bfloat16),
            pltpu.VMEM((Z, Y, CORES, SLOTS, width), jnp.bfloat16),
            pltpu.VMEM((HELD, Z, Y, BLOCK, width), jnp.bfloat16),
            pltpu.VMEM((Z, 1, 128), jnp.float32),
            pltpu.VMEM((Z, 1, 128), jnp.float32),
            pltpu.VMEM((CORES * Y, Z, 1, 128), jnp.float32),
            pltpu.VMEM((HELD, Z, 128), jnp.float32),
            pltpu.VMEM((HELD, PANEL, 128), jnp.float32),
            pltpu.VMEM((PANEL // 128, 1, 128), jnp.float32),
            pltpu.VMEM((Z, 1, 128), jnp.float32),
            pltpu.VMEM((CORES * Y, Z, 1, 128), jnp.float32),
            dma,
            dma((GROUPS,)),
            dma,
            dma((GROUPS,)),
            dma,
            dma((GROUPS,)),
            dma((GROUPS,)),
            dma((3,)),
            dma((3,)),
            dma((2,)),
            dma((2,)),
            dma((3,)),
            pltpu.VMEM((PANEL // 128, 1, 128), jnp.float32),
            pltpu.VMEM((PANEL // 128, 1, 128), jnp.float32),
            dma((2,)),
        ],
        compiler_params=pltpu.CompilerParams(
            collective_id=0, has_side_effects=True, vmem_limit_bytes=48 * 1024 * 1024
        ),
    )(embeddings, cluster, order_rank)
    return found.reshape(rows)


def solution(mesh):
    return jax.shard_map(
        body,
        mesh=mesh,
        in_specs=(P(("dp", "helper"), None), P(("dp", "helper")), P(("dp", "helper"))),
        out_specs=P(("dp", "helper")),
        check_vma=False,
    )
```

time: 122 us -> 82.7 us (0.68)
  Pallas kernels: 119 us -> 79.6 us
    pallas_call x1, Pallas kernels: 119 us -> 79.6 us  [body(): pl.pallas_call(kernel, out_shape=jax.ShapeDtypeStruct((1, rows), jnp.floa...]
where the time goes in v2:
time: 82.7 us; the launch traced here: 82.5 us
  Pallas kernels  79.6 us (96%)
  local copies, waits for them, and re-layouts  2.92 us (4%)
    pallas_call x1, Pallas kernels, body(): pl.pallas_call(kernel, out_shape=jax.ShapeDtypeStruct((1, rows), jnp.floa...  79.6 us
    unnamed x7, local copies, waits for them, and re-layouts  2.92 us

profile of v2, /device:TPU:1, one launch (start us, length us, event | category | flops | bytes accessed | tf_op | source)
XLA Modules:
  0.0 82.5 jit_solution(12030206488204426566)
XLA Ops:
  0.0 0.0 copy-start
  0.0 1.0 %copy-done = bf16[256,768]{1,0:T(8,128)(2,1)S(1)} copy-done((bf16[256,768]{1,0:T(8,128)(2,1)S(1)}, bf16[256,768]{1,0:T(8,128)(2,1)}, u32[]{:S(2)}) %copy-start) | copy-done | bytes 393240
  1.0 0.0 copy-start.1
  1.0 0.7 copy-done.1
  1.7 0.0 copy-start.2
  1.7 0.7 copy-done.2
  2.4 79.6 %shard_map.37 = f32[1,256]{1,0:T(1,128)S(1)} custom-call(bf16[256,768]{1,0:T(8,128)(2,1)S(1)} %copy-done, s32[256]{0:T(256)S(1)} %copy-done.1, s32[256]{0:T(256)S(1)} %copy-done.2), custom_call_target="tpu_custom_call" | custom-call | tf_op jit(solution)/shard_map/pallas_call | solution.py:347
  81.9 0.6 copy.5
Async XLA Ops:
  0.0 1.0 %copy-start = (bf16[256,768]{1,0:T(8,128)(2,1)S(1)}, bf16[256,768]{1,0:T(8,128)(2,1)}, u32[]{:S(2)}) copy-start(bf16[256,768]{1,0:T(8,128)(2,1)} %emb_hbm.1) | copy-start | bytes 1179652
  1.0 0.7 copy-start.1
  1.7 0.7 copy-start.2

commit v3 on v2

--- a/solution.py
+++ b/solution.py
@@ -56,6 +56,7 @@
     key_y,
     key_x,
     key_cols,
+    key_rows,
     result,
     ret_z,
     ret_y,
@@ -214,6 +215,9 @@
     def group(g):
         return pl.ds(SPANS[g][0], SPANS[g][1] - SPANS[g][0])
 
+    def lines(g):
+        return pl.ds(SPANS[g][0] * ROWS_Z, (SPANS[g][1] - SPANS[g][0]) * ROWS_Z)
+
     def to_y(g):
         low, high = SPANS[g]
         low = max(low, 1)
@@ -230,9 +234,9 @@
 
     def to_x(g):
         wait_bytes(landed.at[group(g)], y_recv.at[g])
-        panels[0, group(g)] = landed[group(g)].reshape(-1, Y, BLOCK, width)
-        remote(panels.at[0, group(g)], panels.at[1, group(g)], x_send, x1_recv.at[g], at(dx=1))
-        remote(panels.at[0, group(g)], panels.at[2, group(g)], x_send, x2_recv.at[g], at(dx=-1))
+        panels[0, lines(g)] = landed[group(g)].reshape(-1, width)
+        remote(panels.at[0, lines(g)], panels.at[1, lines(g)], x_send, x1_recv.at[g], at(dx=1))
+        remote(panels.at[0, lines(g)], panels.at[2, lines(g)], x_send, x2_recv.at[g], at(dx=-1))
 
     def key_columns():
         wait_bytes(key_x.at[pl.ds(1, HELD - 1)], key_recv_sem.at[2])
@@ -245,6 +249,8 @@
                 keepdims=True,
             )
             key_cols[p] = jnp.broadcast_to(column, shape).reshape(PANEL, 128)
+        for p in range(HELD - 1):
+            key_rows[p] = jnp.transpose(key_cols[p])[0:1, :]
 
     key_steps = {KEY_STEP: keys_to_y, KEY_STEP + 1: keys_to_x, KEY_STEP + 2: key_columns}
     for step in range(GROUPS + LAG_X):
@@ -260,19 +266,16 @@
     def arrived(low, high):
         for g, (first, last) in enumerate(SPANS):
             if low <= first < high:
-                wait_bytes(panels.at[1, group(g)], x1_recv.at[g])
-                wait_bytes(panels.at[2, group(g)], x2_recv.at[g])
+                wait_bytes(panels.at[1, lines(g)], x1_recv.at[g])
+                wait_bytes(panels.at[2, lines(g)], x2_recv.at[g])
 
     def largest(query, best, tiles):
-        query_keys = jnp.transpose(key_cols[query])[0:1, :]
-
         def tile(step, best):
             p, h = tiles(step)
-            queries = panels[query].reshape(PANEL, width)
-            others = panels[p, pl.ds(h * half, half)].reshape(half * ROWS_Z, width)
-            scores = dot_t(others, queries)
-            other_keys = key_cols[p, pl.ds(h * half * ROWS_Z, half * ROWS_Z), :][:, 0:1]
-            scores = jnp.where(other_keys < query_keys, scores, -1.0)
+            at_rows = pl.ds(h * half * ROWS_Z, half * ROWS_Z)
+            scores = dot_t(panels[p, at_rows, :], panels[query])
+            earlier = key_cols[p, at_rows, :][:, 0:1] < key_rows[query]
+            scores = jnp.where(earlier, scores, -1.0)
             return jnp.maximum(best, jnp.max(scores, axis=0, keepdims=True))
 
         return lambda count: lax.fori_loop(0, count, tile, best)
@@ -299,6 +302,9 @@
             ret_recv_sem.at[0],
             at(dz=-z_offset(a)),
         )
+    spot = a_of * ROWS_Z + dy * BLOCK + core * SLOTS + slot
+    chosen = (iota((128, rows), 0) == spot % 128).astype(jnp.float32)
+    wanted = iota((CORES * Z, rows), 0) == owner_core * Z + a_of
     ret_z[0] = result[0]
     wait_bytes(ret_z.at[pl.ds(1, Z - 1)], ret_recv_sem.at[0])
     for d in range(Y):
@@ -320,13 +326,10 @@
             merged += jnp.where(lane % ROWS_Z // BLOCK == d, ret_y[c * Y + d].reshape(Z, 128), 0.0)
         table.append(merged)
     table = jnp.concatenate(table, axis=0)
-    spot = a_of * ROWS_Z + dy * BLOCK + core * SLOTS + slot
-    chosen = (iota((128, rows), 0) == spot % 128).astype(jnp.float32)
     found = jnp.dot(
         table, chosen, precision=lax.Precision.HIGHEST, preferred_element_type=jnp.float32
     )
-    wanted = owner_core * Z + a_of
-    found = jnp.where(iota((CORES * Z, rows), 0) == wanted, found, 0.0)
+    found = jnp.where(wanted, found, 0.0)
     out_ref[...] = jnp.sum(found, axis=0, keepdims=True)
 
     wait_bytes(from_z.at[pl.ds(1, Z - 1)], z_send)
@@ -357,12 +360,13 @@
             pltpu.VMEM((Z, CORES, Y, SLOTS, width), jnp.bfloat16),
             pltpu.VMEM((Z, CORES, Y, SLOTS, width), jnp.bfloat16),
             pltpu.VMEM((Z, Y, CORES, SLOTS, width), jnp.bfloat16),
-            pltpu.VMEM((HELD, Z, Y, BLOCK, width), jnp.bfloat16),
+            pltpu.VMEM((HELD, PANEL, width), jnp.bfloat16),
             pltpu.VMEM((Z, 1, 128), jnp.float32),
             pltpu.VMEM((Z, 1, 128), jnp.float32),
             pltpu.VMEM((CORES * Y, Z, 1, 128), jnp.float32),
             pltpu.VMEM((HELD, Z, 128), jnp.float32),
             pltpu.VMEM((HELD, PANEL, 128), jnp.float32),
+            pltpu.VMEM((HELD - 1, 1, PANEL), jnp.float32),
             pltpu.VMEM((PANEL // 128, 1, 128), jnp.float32),
             pltpu.VMEM((Z, 1, 128), jnp.float32),
             pltpu.VMEM((CORES * Y, Z, 1, 128), jnp.float32),
@@ -383,7 +387,7 @@
             dma((2,)),
         ],
         compiler_params=pltpu.CompilerParams(
-            collective_id=0, has_side_effects=True, vmem_limit_bytes=48 * 1024 * 1024
+            collective_id=0, has_side_effects=True, vmem_limit_bytes=60 * 1024 * 1024
         ),
     )(embeddings, cluster, order_rank)
     return found.reshape(rows)

time: 82.7 us -> 81.2 us (0.982)
  local copies, waits for them, and re-layouts: 2.92 us -> 1.22 us
    unnamed x7 -> x3, local copies, waits for them, and re-layouts: 2.92 us -> 1.22 us
where the time goes in v3:
time: 81.2 us; the launch traced here: 81.1 us
  Pallas kernels  79.9 us (98%)
  local copies, waits for them, and re-layouts  1.22 us (2%)
    pallas_call x1, Pallas kernels, body(): pl.pallas_call(kernel, out_shape=jax.ShapeDtypeStruct((1, rows), jnp.floa...  79.9 us

profile of v3, /device:TPU:1, one launch (start us, length us, event | category | flops | bytes accessed | tf_op | source)
XLA Modules:
  0.0 81.1 jit_solution(9195047312865336781)
XLA Ops:
  0.0 79.9 %shard_map.37 = f32[1,256]{1,0:T(1,128)} custom-call(bf16[256,768]{1,0:T(8,128)(2,1)} %emb_hbm.1, s32[256]{0:T(256)} %cluster_hbm.1, s32[256]{0:T(256)} %rank_hbm.1), custom_call_target="tpu_custom_call" | custom-call | tf_op jit(solution)/shard_map/pallas_call | solution.py:350
  79.9 0.0 copy-start
  79.9 0.7 copy-done
  80.5 0.6 copy.5
Async XLA Ops:
  79.9 0.7 copy-start

commit v4 on v3

--- a/solution.py
+++ b/solution.py
@@ -15,7 +15,7 @@
 PANEL = Z * ROWS_Z
 SPANS = tuple((low, low + 2) for low in range(0, Z, 2))
 GROUPS = len(SPANS)
-PACE = (-1,) * GROUPS
+NEAR = 8
 KEY_STEP = 2
 LAG_X = 1
 HELD = 3
@@ -75,6 +75,7 @@
     far_send,
     far_recv,
     far_sem,
+    all_in,
 ):
     dp, hx = lax.axis_index("dp"), lax.axis_index("helper")
     core, chip = dp % CORES, dp // CORES
@@ -103,7 +104,7 @@
     for load in loads:
         load.start()
     barrier = pltpu.get_barrier_semaphore()
-    peers = [at(dz=z_offset(a)) for a in range(Z - 1, 0, -1)]
+    peers = [at(dz=z_offset(a)) for a in range(NEAR, 0, -1)]
     peers += [at(dy=d) for d in range(1, Y)] + [at(dy=d, dcore=1) for d in range(Y)]
     peers += [at(dx=1), at(dx=-1)]
     for peer in peers:
@@ -145,11 +146,20 @@
     def group_of(a):
         return next(g for g, (low, high) in enumerate(SPANS) if low <= a < high)
 
-    def release(arrived):
-        for g, (low, high) in enumerate(SPANS):
-            if PACE[g] == arrived:
-                for a in range(max(low, 1), high):
-                    send_rows(a)
+    def release(first, last):
+        for a in range(first, last):
+            send_key(a)
+        for a in range(first, last):
+            send_rows(a)
+
+    def send_key(a):
+        remote(
+            key_send.at[a],
+            key_z.at[a],
+            key_send_sem.at[0],
+            key_recv_sem.at[0],
+            at(dz=z_offset(a)),
+        )
 
     def send_rows(a):
         remote(
@@ -168,15 +178,12 @@
     key_send[...] = keys.reshape(Z, 1, 128)
     key_z[0] = keys[0:1]
     pl.semaphore_wait(barrier, len(peers))
-    for a in range(1, Z):
-        remote(
-            key_send.at[a],
-            key_z.at[a],
-            key_send_sem.at[0],
-            key_recv_sem.at[0],
-            at(dz=z_offset(a)),
-        )
-    release(-1)
+    for dz in (Z // 4, -(Z // 4)):
+        pl.semaphore_signal(all_in, inc=1, device_id=at(dz=dz), device_id_type=MESH)
+    release(1, NEAR + 1)
+    pl.semaphore_wait(all_in, 2)
+    release(NEAR + 1, Z)
+
     lane = iota((Z, 128), 1)
 
     def keys_to_y():
@@ -222,7 +229,6 @@
         low, high = SPANS[g]
         low = max(low, 1)
         wait_bytes(from_z.at[pl.ds(low, high - low)], z_recv.at[g])
-        release(g)
         for d in range(Y):
             for other in range(CORES):
                 src = from_z.at[group(g), (core + other) % CORES, d]
@@ -385,6 +391,7 @@
             pltpu.VMEM((PANEL // 128, 1, 128), jnp.float32),
             pltpu.VMEM((PANEL // 128, 1, 128), jnp.float32),
             dma((2,)),
+            pltpu.SemaphoreType.REGULAR,
         ],
         compiler_params=pltpu.CompilerParams(
             collective_id=0, has_side_effects=True, vmem_limit_bytes=60 * 1024 * 1024

time: 81.2 us -> 78.5 us (0.967)
  Pallas kernels: 79.9 us -> 77.1 us
    pallas_call x1, Pallas kernels: 79.9 us -> 77.1 us  [body(): pl.pallas_call(kernel, out_shape=jax.ShapeDtypeStruct((1, rows), jnp.floa...]
where the time goes in v4:
time: 78.5 us; the launch traced here: 78.3 us
  Pallas kernels  77.1 us (98%)
  local copies, waits for them, and re-layouts  1.22 us (2%)
    pallas_call x1, Pallas kernels, body(): pl.pallas_call(kernel, out_shape=jax.ShapeDtypeStruct((1, rows), jnp.floa...  77.1 us

profile of v4, /device:TPU:1, one launch (start us, length us, event | category | flops | bytes accessed | tf_op | source)
XLA Modules:
  0.0 78.3 jit_solution(3183324919019964160)
XLA Ops:
  0.0 77.1 %shard_map.37 = f32[1,256]{1,0:T(1,128)} custom-call(bf16[256,768]{1,0:T(8,128)(2,1)} %emb_hbm.1, s32[256]{0:T(256)} %cluster_hbm.1, s32[256]{0:T(256)} %rank_hbm.1), custom_call_target="tpu_custom_call" | custom-call | tf_op jit(solution)/shard_map/pallas_call | solution.py:356
  77.1 0.0 copy-start
  77.1 0.7 copy-done
  77.8 0.6 copy.5
Async XLA Ops:
  77.1 0.7 copy-start

commit v5 on v4

--- a/solution.py
+++ b/solution.py
@@ -16,6 +16,7 @@
 SPANS = tuple((low, low + 2) for low in range(0, Z, 2))
 GROUPS = len(SPANS)
 NEAR = 8
+FAR_FIRST = (2, 1, 3, 0)
 KEY_STEP = 2
 LAG_X = 1
 HELD = 3
@@ -229,8 +230,8 @@
         low, high = SPANS[g]
         low = max(low, 1)
         wait_bytes(from_z.at[pl.ds(low, high - low)], z_recv.at[g])
-        for d in range(Y):
-            for other in range(CORES):
+        for d in FAR_FIRST:
+            for other in (1, 0):
                 src = from_z.at[group(g), (core + other) % CORES, d]
                 dst = landed.at[group(g), d, core]
                 if d or other:
@@ -313,8 +314,8 @@
     wanted = iota((CORES * Z, rows), 0) == owner_core * Z + a_of
     ret_z[0] = result[0]
     wait_bytes(ret_z.at[pl.ds(1, Z - 1)], ret_recv_sem.at[0])
-    for d in range(Y):
-        for other in range(CORES):
+    for d in FAR_FIRST:
+        for other in (1, 0):
             if d or other:
                 remote(
                     ret_z,

time: 78.5 us -> 78.1 us (level)
  no operation moved by 1% of the time
where the time goes in v5:
time: 78.1 us; the launch traced here: 78 us
  Pallas kernels  76.7 us (98%)
  local copies, waits for them, and re-layouts  1.22 us (2%)
    pallas_call x1, Pallas kernels, body(): pl.pallas_call(kernel, out_shape=jax.ShapeDtypeStruct((1, rows), jnp.floa...  76.7 us

profile of v5, /device:TPU:1, one launch (start us, length us, event | category | flops | bytes accessed | tf_op | source)
XLA Modules:
  0.0 78.0 jit_solution(12503041948535122428)
XLA Ops:
  0.0 76.7 %shard_map.37 = f32[1,256]{1,0:T(1,128)} custom-call(bf16[256,768]{1,0:T(8,128)(2,1)} %emb_hbm.1, s32[256]{0:T(256)} %cluster_hbm.1, s32[256]{0:T(256)} %rank_hbm.1), custom_call_target="tpu_custom_call" | custom-call | tf_op jit(solution)/shard_map/pallas_call | solution.py:357
  76.7 0.0 copy-start
  76.7 0.7 copy-done
  77.4 0.6 copy.5
Async XLA Ops:
  76.7 0.7 copy-start

commit v6 on v5

--- a/solution.py
+++ b/solution.py
@@ -15,7 +15,7 @@
 PANEL = Z * ROWS_Z
 SPANS = tuple((low, low + 2) for low in range(0, Z, 2))
 GROUPS = len(SPANS)
-NEAR = 8
+NEAR = 4
 FAR_FIRST = (2, 1, 3, 0)
 KEY_STEP = 2
 LAG_X = 1
@@ -76,7 +76,7 @@
     far_send,
     far_recv,
     far_sem,
-    all_in,
+    wider,
 ):
     dp, hx = lax.axis_index("dp"), lax.axis_index("helper")
     core, chip = dp % CORES, dp // CORES
@@ -179,11 +179,16 @@
     key_send[...] = keys.reshape(Z, 1, 128)
     key_z[0] = keys[0:1]
     pl.semaphore_wait(barrier, len(peers))
-    for dz in (Z // 4, -(Z // 4)):
-        pl.semaphore_signal(all_in, inc=1, device_id=at(dz=dz), device_id_type=MESH)
-    release(1, NEAR + 1)
-    pl.semaphore_wait(all_in, 2)
-    release(NEAR + 1, Z)
+    first, reach = 1, NEAR // 2
+    for step in range(2):
+        for dz in (reach, -reach):
+            pl.semaphore_signal(
+                wider.at[step], inc=1, device_id=at(dz=dz), device_id_type=MESH
+            )
+        release(first, 2 * reach + 1)
+        pl.semaphore_wait(wider.at[step], 2)
+        first, reach = 2 * reach + 1, 2 * reach
+    release(first, Z)
 
     lane = iota((Z, 128), 1)
 
@@ -392,7 +397,7 @@
             pltpu.VMEM((PANEL // 128, 1, 128), jnp.float32),
             pltpu.VMEM((PANEL // 128, 1, 128), jnp.float32),
             dma((2,)),
-            pltpu.SemaphoreType.REGULAR,
+            pltpu.SemaphoreType.REGULAR((2,)),
         ],
         compiler_params=pltpu.CompilerParams(
             collective_id=0, has_side_effects=True, vmem_limit_bytes=60 * 1024 * 1024

time: 78.1 us -> 78 us (level)
  no operation moved by 1% of the time
where the time goes in v6:
time: 78 us; the launch traced here: 77.9 us
  Pallas kernels  76.7 us (98%)
  local copies, waits for them, and re-layouts  1.22 us (2%)
    pallas_call x1, Pallas kernels, body(): pl.pallas_call(kernel, out_shape=jax.ShapeDtypeStruct((1, rows), jnp.floa...  76.7 us

profile of v6, /device:TPU:1, one launch (start us, length us, event | category | flops | bytes accessed | tf_op | source)
XLA Modules:
  0.0 77.9 jit_solution(8744890325730013087)
XLA Ops:
  0.0 76.7 %shard_map.37 = f32[1,256]{1,0:T(1,128)} custom-call(bf16[256,768]{1,0:T(8,128)(2,1)} %emb_hbm.1, s32[256]{0:T(256)} %cluster_hbm.1, s32[256]{0:T(256)} %rank_hbm.1), custom_call_target="tpu_custom_call" | custom-call | tf_op jit(solution)/shard_map/pallas_call | solution.py:362
  76.7 0.0 copy-start
  76.7 0.7 copy-done
  77.3 0.6 copy.5
Async XLA Ops:
  76.7 0.7 copy-start
